TPU v7x, 512 devices: a whole 4x4x16 slice. The times are simulated.
512 devices in a mesh: node: 16 (over y, z_hi, core), group: 32 (over x, z_lo).
Axes of the slice: x: 4, y: 4, z: 16 (z_hi: 2, z_lo: 8; z = z_hi * 8 + z_lo), core: 2. Of those that a mesh axis runs over, the one named last changes fastest.
Arguments:
- residual: bfloat16 [98304, 5120], P(('node', 'group')), may hold values from -24 to 24
- norm_gain_vector: float32 [5120], replicated, may hold values from 0.3 to 3
- key_projection_matrix: bfloat16 [5120, 512], P('node'), may hold values from -0.078125 to 0.078125
- key_output_gradient: bfloat16 [98304, 512], P(('node', 'group')), may hold values from -6 to 6
Outputs:
- residual_gradient: bfloat16 [98304, 5120], P(('node', 'group'))
- weight_grad: float32 [5120, 512], P(('node', 'group'))
All inputs are finite; a program needn't handle non-finite values.
Results may differ from a plain program's by a relative error of at most 0.017.
Values may be sent and summed in bfloat16 or wider, within the bound.
A program may use at most 128 MiB of HBM per device.

v0:
```python
import jax
import jax.numpy as jnp
from jax import lax
from jax.sharding import PartitionSpec as P


def quantize_blocks(blocks):
    scales = ((jnp.max(jnp.abs(blocks), axis=2, keepdims=True) + 1e-06) / 127.0).astype(
        jnp.bfloat16
    )
    tiles = (blocks / scales.astype(jnp.float32)).astype(jnp.bfloat16)
    return (tiles, scales)


def restore_sum(tiles, scales, count):
    rows = tiles.shape[0] // count
    value_entries = tiles.reshape((count, rows, tiles.shape[1], tiles.shape[2])).astype(jnp.float32)
    factors = scales.reshape((count, rows, scales.shape[1], scales.shape[2])).astype(jnp.float32)
    return jnp.sum(value_entries * factors, axis=0)


def group_section(first):
    tiles_two, scales_two = quantize_blocks(first)
    more_tiles, more_scales = (
        lax.all_to_all(tiles_two, "group", split_axis=0, concat_axis=0, tiled=True),
        lax.all_to_all(scales_two, "group", split_axis=0, concat_axis=0, tiled=True),
    )
    return restore_sum(more_tiles, more_scales, lax.axis_size("group"))


def weight_path(normed_input, key_output_gradient, tokens_all):
    partial_value = lax.dot_general(
        normed_input,
        key_output_gradient,
        (((0,), (0,)), ((), ())),
        preferred_element_type=jnp.float32,
    )
    width = partial_value.shape[1]
    tiles, scales = quantize_blocks(
        partial_value.reshape((partial_value.shape[0], width // 128, 128))
    )
    got_tiles, got_scales = (
        lax.all_to_all(tiles, "node", split_axis=0, concat_axis=0, tiled=True),
        lax.all_to_all(scales, "node", split_axis=0, concat_axis=0, tiled=True),
    )
    total = group_section(restore_sum(got_tiles, got_scales, lax.axis_size("node")))
    return total.reshape((total.shape[0], width)) * float(tokens_all) ** (-0.5)


def input_route(
    unit_input, root_mean_square, norm_gain_vector, key_projection_matrix, key_output_gradient
):
    feature_grad = lax.dot_general(
        key_output_gradient,
        lax.all_gather(key_projection_matrix, "node", axis=0, tiled=True),
        (((1,), (1,)), ((), ())),
        preferred_element_type=jnp.float32,
    )
    scaled_input = feature_grad * norm_gain_vector[None, :]
    inner_function = jnp.mean(scaled_input * unit_input, axis=1, keepdims=True)
    return ((scaled_input - unit_input * inner_function) / root_mean_square).astype(jnp.bfloat16)


def on_device(residual, norm_gain_vector, key_projection_matrix, key_output_gradient):
    value_entries = residual.astype(jnp.float32)
    root_mean_square = jnp.sqrt(
        jnp.mean(value_entries * value_entries, axis=1, keepdims=True) + 1e-06
    )
    unit_input = value_entries / root_mean_square
    normed_input = (unit_input * norm_gain_vector[None, :]).astype(jnp.bfloat16)
    tokens_all = residual.shape[0] * lax.axis_size("node") * lax.axis_size("group")
    weight_grad = weight_path(normed_input, key_output_gradient, tokens_all)
    residual_gradient = input_route(
        unit_input, root_mean_square, norm_gain_vector, key_projection_matrix, key_output_gradient
    )
    return (residual_gradient, weight_grad)


def solution(mesh):
    return jax.shard_map(
        on_device,
        mesh=mesh,
        in_specs=(P(("node", "group"), None), P(), P("node", None), P(("node", "group"), None)),
        out_specs=(P(("node", "group"), None), P(("node", "group"), None)),
        check_vma=False,
    )
```

profile of v0, /device:TPU:1, one launch (start us, length us, event | category | flops | bytes accessed | tf_op | source)
XLA Modules:
  0.0 521.1 jit_solution(9311519827241176204)
XLA Ops:
  7.2 2.1 fusion.1
  9.3 7.3 %abs_reduce_fusion = (f32[5120,4]{0,1:T(4,128)S(1)}, f32[5120,512]{0,1:T(8,128)}) fusion(bf16[192,512]{1,0:T(8,128)(2,1)S(1)} %copy-done, f32[5120]{0:T(1024)} %param.5, f32[192]{0:T(256)S(1)} %add_sqrt_fusion, bf16[192,5120]{1,0:T(8,128)(2,1)} %param.4), kind=kOutput, calls=%fused_computation.2 | convolution fusion | flops 1015787520 | bytes 12751616 | tf_op jit(solution)/shard_map/dot_general | solution.py:32
  16.6 2.0 copy.35
  19.1 28.9 %reduce = bf16[5120,4]{1,0:T(8,128)(2,1)} reduce(bf16[5120,1,4]{2,1,0:T(2,128)(2,1)S(1)} %bitcast.25, bf16[]{:T(256)} %broadcast.80), dimensions={1}, to_apply=%bitcast.16.reduce_sub_computation | reduce | bytes 81922
  48.0 4.0 reshape.104
  52.0 19.2 %all-to-all-start.1 = ((bf16[16,2,640]{2,1,0:T(2,128)(2,1)}), bf16[16,2,640]{2,1,0:T(2,128)(2,1)S(1)}, u32[]{:S(2)}, u32[]{:S(2)}) async-start(bf16[16,2,640]{2,1,0:T(2,128)(2,1)} %reshape.104), calls=%async_computation.1 | async-start | bytes 81920 | tf_op jit(solution)/shard_map/all_to_all | solution.py:44
  71.3 12.2 %copy.33 = f32[5120,4,128]{2,1,0:T(4,128)} copy(f32[5120,4,128]{0,2,1:T(8,128)} %bitcast.23) | data formatting | bytes 20971520 | tf_op jit(solution)/shard_map/reshape | solution.py:40
  83.5 0.8 copy.32
  84.2 14.1 %divide_convert_fusion = bf16[5120,4,128]{2,1,0:T(4,128)(2,1)} fusion(f32[5120,4,128]{2,1,0:T(4,128)} %copy.33, f32[5120,4]{1,0:T(8,128)S(1)} %copy.32), kind=kLoop, calls=%fused_computation.3 | loop fusion | flops 5242880 | bytes 15810560 | tf_op jit(solution)/shard_map/convert_element_type | solution.py:11
  98.4 14.4 %all-to-all-start = ((bf16[5120,4,128]{2,1,0:T(4,128)(2,1)}), bf16[5120,4,128]{2,1,0:T(4,128)(2,1)}, u32[]{:S(2)}, u32[]{:S(2)}) async-start(bf16[5120,4,128]{2,1,0:T(4,128)(2,1)} %divide_convert_fusion), calls=%async_computation | async-start | bytes 10485760 | tf_op jit(solution)/shard_map/all_to_all | solution.py:43
  113.5 3.3 reshape.105
  116.9 4.0 bitcast_convert_fusion
  120.9 2.7 copy.36
  123.6 307.9 %all-gather.2.cloned.1.call-done = bf16[5120,512]{1,0:T(8,128)(2,1)} async-done(((bf16[320,512]{1,0:T(8,128)(2,1)}), bf16[5120,512]{1,0:T(8,128)(2,1)}) %all-gather.2.cloned.1.call-update) | async-done | bytes 5242896 | tf_op jit(solution)/shard_map/all_gather | solution.py:55
  431.5 6.9 %multiply_reduce_fusion = (f32[192]{0:T(256)S(1)}, f32[192,5120]{1,0:T(8,128)}) fusion(f32[192]{0:T(256)S(1)} %add_sqrt_fusion, bf16[192,5120]{1,0:T(8,128)(2,1)} %param.4, f32[5120]{0:T(1024)S(1)} %copy-done.2, bf16[192,512]{1,0:T(8,128)(2,1)S(1)} %copy-done, bf16[5120,512]{1,0:T(8,128)(2,1)} %all-gather.2.cloned.1.call-done), kind=kOutput, calls=%fused_computation.10 | convolution fusion | flops 1011547968 | bytes 11359744 | tf_op jit(solution)/shard_map/dot_general | solution.py:53
  438.4 3.2 copy.34
  441.6 3.2 fusion
  445.0 0.8 copy.38
  445.9 25.7 %all-to-all-start.3 = ((bf16[320,4,1]{1,2,0:T(2,128)(2,1)}), bf16[320,4,1]{1,2,0:T(2,128)(2,1)S(1)}, u32[]{:S(2)}, u32[]{:S(2)}) async-start(bf16[320,4,1]{1,2,0:T(2,128)(2,1)} %copy.38), calls=%async_computation.3 | async-start | bytes 327680 | tf_op jit(solution)/shard_map/all_to_all | solution.py:26
  471.8 1.0 copy.37
  472.8 11.1 %all-to-all-done.3 = bf16[320,4,1]{1,2,0:T(2,128)(2,1)S(1)} async-done(((bf16[320,4,1]{1,2,0:T(2,128)(2,1)}), bf16[320,4,1]{1,2,0:T(2,128)(2,1)S(1)}, u32[]{:S(2)}, u32[]{:S(2)}) %all-to-all-start.3) | async-done | bytes 2592 | tf_op jit(solution)/shard_map/all_to_all | solution.py:26
  483.9 7.9 %all-to-all-start.2 = ((bf16[320,4,128]{2,1,0:T(4,128)(2,1)}), bf16[320,4,128]{2,1,0:T(4,128)(2,1)S(1)}, u32[]{:S(2)}, u32[]{:S(2)}) async-start(bf16[320,4,128]{2,1,0:T(4,128)(2,1)} %copy.37), calls=%async_computation.2 | async-start | bytes 655360 | tf_op jit(solution)/shard_map/all_to_all | solution.py:25
  491.8 4.4 divide_convert_fusion.1
  496.7 16.5 %all-to-all-done.2 = bf16[320,4,128]{2,1,0:T(4,128)(2,1)S(1)} async-done(((bf16[320,4,128]{2,1,0:T(4,128)(2,1)}), bf16[320,4,128]{2,1,0:T(4,128)(2,1)S(1)}, u32[]{:S(2)}, u32[]{:S(2)}) %all-to-all-start.2) | async-done | bytes 327712 | tf_op jit(solution)/shard_map/all_to_all | solution.py:25
  (24 shorter events, 3.4 us)
Async XLA Ops:
  7.2 2.1 copy-start
  52.0 46.3 %all-to-all-start.1 = ((bf16[16,2,640]{2,1,0:T(2,128)(2,1)}), bf16[16,2,640]{2,1,0:T(2,128)(2,1)S(1)}, u32[]{:S(2)}, u32[]{:S(2)}) async-start(bf16[16,2,640]{2,1,0:T(2,128)(2,1)} %reshape.104), calls=%async_computation.1 | async-start | bytes 81920 | tf_op jit(solution)/shard_map/all_to_all | solution.py:44
  98.4 340.0 %all-to-all-start = ((bf16[5120,4,128]{2,1,0:T(4,128)(2,1)}), bf16[5120,4,128]{2,1,0:T(4,128)(2,1)}, u32[]{:S(2)}, u32[]{:S(2)}) async-start(bf16[5120,4,128]{2,1,0:T(4,128)(2,1)} %divide_convert_fusion), calls=%async_computation | async-start | bytes 10485760 | tf_op jit(solution)/shard_map/all_to_all | solution.py:43
  112.8 318.7 %all-gather.2.cloned.1.call-start = ((), (), s32[]{:S(2)}) async-start(), calls=%async_computation.4 | async-start | bytes 5570560 | tf_op jit(solution)/shard_map/all_gather | solution.py:55
  116.9 314.6 %copy-start.2 = (f32[5120]{0:T(1024)S(1)}, f32[5120]{0:T(1024)}, u32[]{:S(2)}) copy-start(f32[5120]{0:T(1024)} %param.5) | copy-start | bytes 61444
  441.6 50.3 %copy-start.1 = (bf16[192,5120]{1,0:T(8,128)(2,1)S(1)}, bf16[192,5120]{1,0:T(8,128)(2,1)}, u32[]{:S(2)}) copy-start(bf16[192,5120]{1,0:T(8,128)(2,1)} %param.4) | copy-start | bytes 5898244
  445.9 38.0 %all-to-all-start.3 = ((bf16[320,4,1]{1,2,0:T(2,128)(2,1)}), bf16[320,4,1]{1,2,0:T(2,128)(2,1)S(1)}, u32[]{:S(2)}, u32[]{:S(2)}) async-start(bf16[320,4,1]{1,2,0:T(2,128)(2,1)} %copy.38), calls=%async_computation.3 | async-start | bytes 327680 | tf_op jit(solution)/shard_map/all_to_all | solution.py:26
  483.9 29.3 %all-to-all-start.2 = ((bf16[320,4,128]{2,1,0:T(4,128)(2,1)}), bf16[320,4,128]{2,1,0:T(4,128)(2,1)S(1)}, u32[]{:S(2)}, u32[]{:S(2)}) async-start(bf16[320,4,128]{2,1,0:T(4,128)(2,1)} %copy.37), calls=%async_computation.2 | async-start | bytes 655360 | tf_op jit(solution)/shard_map/all_to_all | solution.py:25
Sparse Core Ops, SparseCore 0:
  116.9 314.5 all-gather.1
where the time goes:
time: 522 us; the launch traced here: 521 us
  waiting for transfers between devices  336 us (64%)
  starting transfers between devices  67.3 us (13%)
  other arithmetic  57.6 us (11%)
  local copies, waits for them, and re-layouts  31.6 us (6%)
  matrix products  14.2 us (3%)
  between operations  14.2 us (3%)
    all_gather x1, waiting for transfers between devices, input_route(): lax.all_gather(key_projection_matrix, 'node', axis=0, tiled=True)  308 us
    unnamed x1, other arithmetic  28.9 us
    all_to_all x1, starting transfers between devices, group_section(): lax.all_to_all(scales_two, 'group', split_axis=0, concat_axis=0, tiled=True)  25.7 us
    all_to_all x1, starting transfers between devices, weight_path(): lax.all_to_all(scales, 'node', split_axis=0, concat_axis=0, tiled=True)  19.2 us
    all_to_all x1, waiting for transfers between devices, group_section(): lax.all_to_all(tiles_two, 'group', split_axis=0, concat_axis=0, tiled=True)  16.5 us
    all_to_all x1, starting transfers between devices, weight_path(): lax.all_to_all(tiles, 'node', split_axis=0, concat_axis=0, tiled=True)  14.4 us
    convert_element_type x2, other arithmetic, quantize_blocks(): tiles = (blocks / scales.astype(jnp.float32)).astype(jnp.bfloat16)  14.3 us
    reshape x1, local copies, waits for them, and re-layouts, weight_path(): partial_value.reshape((partial_value.shape[0], width // 128, 128))  12.2 us
  transfers between devices with their start and end apart: 5, of which 3 were waited for; matrix products, arithmetic and copies ran while one was open for 10% of the time, Pallas kernels for 0%

commit v1 on v0

v1 whole, which is shorter than its diff:
```python
import jax
import jax.numpy as jnp
from jax import lax
from jax.experimental import pallas as pl
from jax.experimental.pallas import tpu as pltpu
from jax.sharding import PartitionSpec as P

MESH = pl.DeviceIdType.MESH
F32, BF16 = jnp.float32, jnp.bfloat16

RING = 4
DEPTH = 16
Z_LO = 8
ORDER = (2, 1, 3, 0)


def place():
    n, g = lax.axis_index("node"), lax.axis_index("group")
    return g // Z_LO, n // 4, (n // 2) % 2 * Z_LO + g % Z_LO, n % 2


def device(x, y, z, c):
    return (y * 4 + z // Z_LO * 2 + c, x * Z_LO + z % Z_LO)


def kernel(
    res_hbm,
    grad_hbm,
    w_hbm,
    gain_ref,
    out_hbm,
    wg_ref,
    res,
    grad,
    both_res,
    both_grad,
    product,
    send1,
    recv1,
    red,
    recv2,
    acc,
    send3,
    recv3,
    w,
    scaled,
    rinv_ref,
    dot_ref,
    out,
    local_sem,
    pair_sem,
    one_sem,
    two_sem,
    three_sem,
    wz_sem,
    wa_sem,
    wb_sem,
    wx_sem,
    wc_sem,
    out_sem,
):
    x, y, z, c = place()
    zh = z // Z_LO
    tokens, width = res.shape
    shard = w_hbm.shape[0]
    quarter = shard // RING
    rows = quarter // Z_LO
    first, second = x + c * (y - x), y + c * (x - y)
    other = device(x, y, z, 1 - c)

    def along_first(d):
        return device((x + (1 - c) * d) % RING, (y + c * d) % RING, z, c)

    def along_second(d):
        return device((x + c * d) % RING, (y + (1 - c) * d) % RING, z, c)

    def along_x(d):
        return device((x + d) % RING, y, z, c)

    def along_y(d):
        return device(x, (y + d) % RING, z, c)

    def along_z(d):
        return device(x, y, (z + d) % DEPTH, c)

    def remote(src, dst, sems, index, target):
        return pltpu.make_async_remote_copy(
            src_ref=src,
            dst_ref=dst,
            send_sem=sems.at[(0, *index)],
            recv_sem=sems.at[(1, *index)],
            device_id=target,
            device_id_type=MESH,
        )

    barrier = pltpu.get_barrier_semaphore()
    partners = (
        [along_z(d) for d in (8, 7, 9, 6, 10, 5, 11, 4, 12, 3, 13, 2, 14, 1, 15)]
        + [along_x(d) for d in (1, 2, 3)]
        + [along_y(d) for d in (1, 2, 3)]
        + [other]
    )
    for partner in partners:
        pl.semaphore_signal(barrier, inc=1, device_id=partner, device_id_type=MESH)

    def w_rows(yy, hi, core, count=shard, at=0):
        start = ((yy * 2 + hi) * 2 + core) * shard + at
        return w.at[pl.ds(pl.multiple_of(start, 16), count)]

    def columns(block, core):
        start = block * (2 * shard) + core * 256
        return res_hbm.at[:, pl.ds(pl.multiple_of(start, 128), 384)]

    mine = pl.ds(pl.multiple_of(c * tokens, 16), tokens)
    load_res = pltpu.make_async_copy(res_hbm, res, local_sem.at[0])
    load_grad = pltpu.make_async_copy(grad_hbm, grad, local_sem.at[1])
    load_w = pltpu.make_async_copy(w_hbm, w_rows(y, zh, c), local_sem.at[2])
    load_pair = [
        pltpu.make_async_copy(columns(b, c), both_res.at[b, mine], local_sem.at[3 + b])
        for b in range(8)
    ]
    load_res.start()
    load_grad.start()
    for b in range(8):
        load_pair[b].start()
    load_w.start()
    load_grad.wait()
    load_res.wait()

    def norm(i, carry):
        at = pl.ds(pl.multiple_of(i * 16, 16), 16)
        v = res[at].astype(F32)
        rms = jnp.sqrt(jnp.sum(v * v, axis=1, keepdims=True) / width + 1e-06)
        rinv = 1.0 / rms
        rinv_ref[at] = jnp.broadcast_to(rinv, (16, 128))
        both_grad[pl.ds(pl.multiple_of(c * tokens + i * 16, 16), 16)] = (
            grad[at].astype(F32) * rinv
        ).astype(BF16)
        return carry

    lax.fori_loop(0, tokens // 16, norm, 0)

    pl.semaphore_wait(barrier, len(partners))

    swap_grad = remote(both_grad.at[mine], both_grad.at[mine], pair_sem, (8,), other)
    swap_res = [
        remote(columns(b, 1 - c), both_res.at[b, mine], pair_sem, (b,), other) for b in range(8)
    ]
    swap_grad.start()
    for b in range(8):
        swap_res[b].start()

    w_far = remote(
        w_hbm.at[pl.ds(pl.multiple_of(x * quarter, 16), quarter)],
        w_rows(y, zh, c, quarter, x * quarter),
        wz_sem,
        (0,),
        along_z(8),
    )
    w_far.start()
    w_near = {d: remote(w_hbm, w_rows(y, zh, c), wa_sem, (d - 1,), along_y(d)) for d in (1, 2, 3)}
    w_near[1].start()
    w_near[3].start()
    load_w.wait()

    def to_other(yy, hi):
        return remote(
            w_rows(yy, hi, c), w_rows(yy, hi, c), wc_sem, (yy * 2 + hi,), other
        )

    to_other(y, zh).start()

    for b in range(8):
        load_pair[b].wait()
    swap_grad.wait_recv()
    for b in range(8):
        swap_res[b].wait_recv()

    def copy_one(d, s):
        return remote(
            send1.at[(first + d) % RING, s], recv1.at[d - 1, s], one_sem, (d - 1, s), along_first(d)
        )

    def partial_block(yy):
        def half(hi, carry):
            product[...] = lax.dot_general(
                both_res[yy * 2 + hi],
                both_grad[...],
                (((0,), (0,)), ((), ())),
                preferred_element_type=F32,
            )
            for q in range(RING):
                at = pl.ds(pl.multiple_of(c * 64 + q * quarter, 16), quarter)
                send1[
                    q + c * (yy - q), yy + c * (q - yy), pl.ds(pl.multiple_of(hi * quarter, 16), quarter)
                ] = product[at].astype(BF16)
            return carry

        lax.fori_loop(0, 2, half, 0)

    for step in ORDER:
        yy = (y + step) % RING
        partial_block(yy)

        @pl.when(c == 0)
        def _(yy=yy):
            for d in (2, 1, 3):
                copy_one(d, yy).start()

    @pl.when(c == 1)
    def _():
        for step in ORDER:
            for d in (2, 1, 3):
                copy_one(d, (x + step) % RING).start()

    w_far.wait_recv()
    lo = 1 - zh

    def w_side(d):
        piece = w_rows(y, lo, c, quarter, x * quarter)
        return remote(piece, piece, wb_sem, (d - 1,), along_y(d))

    for d in (2, 1, 3):
        w_side(d).start()

    def copy_two(e):
        return remote(red.at[(second + e) % RING], recv2.at[e - 1], two_sem, (e - 1,), along_second(e))

    for step in ORDER:
        s = (second + step) % RING
        for d in (1, 2, 3):
            copy_one(d, s).wait_recv()

        def add(i, carry, s=s, step=step):
            at = pl.ds(pl.multiple_of(i * 16, 16), 16)
            total = send1[first, s, at].astype(F32)
            for k in range(3):
                total = total + recv1[k, s, at].astype(F32)
            if step:
                red[s, at] = total.astype(BF16)
            else:
                acc[at] = total
            return carry

        lax.fori_loop(0, 2 * quarter // 16, add, 0)
        if step:
            copy_two(step).start()

    def w_across(d, yy):
        piece = w_rows(yy, lo, c, quarter, x * quarter)
        return remote(piece, piece, wx_sem, (d - 1, yy), along_x(d))

    for d in (1, 2, 3):
        w_side(d).wait_recv()
    for yy in range(RING):
        for d in (2, 1, 3):
            w_across(d, yy).start()
    w_near[2].start()

    dot_ref[...] = jnp.zeros_like(dot_ref)

    def features(block):
        at = pl.ds(pl.multiple_of(block * (2 * shard), 128), 2 * shard)
        value = lax.dot_general(
            grad[...],
            w[pl.ds(pl.multiple_of(block * (2 * shard), 16), 2 * shard)],
            (((1,), (1,)), ((), ())),
            preferred_element_type=F32,
        )
        value = value * gain_ref[:, at]
        scaled[:, at] = value
        dot_ref[...] += jnp.sum(value * res[:, at].astype(F32), axis=1, keepdims=True)

    def from_other(yy, hi):
        remote(
            w_rows(yy, hi, 1 - c), w_rows(yy, hi, 1 - c), wc_sem, (yy * 2 + hi,), other
        ).wait_recv()

    for d in (1, 3):
        w_near[d].wait_recv()
        to_other((y + RING - d) % RING, zh).start()
    for d in (0, 1, 3):
        yy = (y + RING - d) % RING
        from_other(yy, zh)
        features(yy * 2 + zh)

    for e in (1, 3, 2):
        copy_two(e).wait_recv()

    def add_two(i, carry):
        at = pl.ds(pl.multiple_of(i * 16, 16), 16)
        total = acc[at]
        for k in range(3):
            total = total + recv2[k, at].astype(F32)
        acc[at] = total
        return carry

    lax.fori_loop(0, 2 * quarter // 16, add_two, 0)
    acc[2 * quarter :] = jnp.zeros((acc.shape[0] - 2 * quarter, acc.shape[1]), F32)
    for k in range(DEPTH):
        send3[k] = acc[k * rows : k * rows + 16].astype(BF16)

    def copy_three(d):
        return remote(send3.at[(z + d) % DEPTH], recv3.at[d - 1], three_sem, (d - 1,), along_z(d))

    distances = (8, 7, 9, 6, 10, 5, 11, 4, 12, 3, 13, 2, 14, 1, 15)
    for d in distances:
        copy_three(d).start()

    w_near[2].wait_recv()
    to_other((y + 2) % RING, zh).start()
    from_other((y + 2) % RING, zh)
    features((y + 2) % RING * 2 + zh)

    for yy in range(RING):
        for d in (1, 2, 3):
            w_across_in = w_rows(yy, lo, c, quarter, (x + RING - d) % RING * quarter)
            remote(w_across_in, w_across_in, wx_sem, (d - 1, yy), along_x(d)).wait_recv()
        to_other(yy, lo).start()
    for yy in range(RING):
        from_other(yy, lo)
        features(yy * 2 + lo)

    def finish(i, carry):
        at = pl.ds(pl.multiple_of(i * 16, 16), 16)
        rinv = rinv_ref[at][:, :1]
        factor = dot_ref[at][:, :1] * (1.0 / width) * rinv * rinv
        out[at] = ((scaled[at] - res[at].astype(F32) * factor) * rinv).astype(BF16)
        return carry

    lax.fori_loop(0, tokens // 16, finish, 0)
    store = pltpu.make_async_copy(out, out_hbm, out_sem.at[0])
    store.start()

    for d in distances:
        copy_three(d).wait_recv()
    total = send3[z].astype(F32)
    for k in range(DEPTH - 1):
        total = total + recv3[k].astype(F32)
    wg_ref[...] = total

    swap_grad.wait_send()
    for b in range(8):
        swap_res[b].wait_send()
    w_far.wait_send()
    for d in (1, 2, 3):
        w_near[d].wait_send()
        w_side(d).wait_send()
        copy_two(d).wait_send()
        for s in range(RING):
            copy_one(d, s).wait_send()
            w_across(d, s).wait_send()
    for yy in range(RING):
        for hi in range(2):
            to_other(yy, hi).wait_send()
    for d in distances:
        copy_three(d).wait_send()
    store.wait()


def on_device(residual, norm_gain_vector, key_projection_matrix, key_output_gradient):
    tokens, width = residual.shape
    features = key_output_gradient.shape[1]
    shard = key_projection_matrix.shape[0]
    quarter = shard // RING
    hbm = pl.BlockSpec(memory_space=pl.ANY)
    vmem = pl.BlockSpec(memory_space=pltpu.VMEM)
    residual_gradient, sums = pl.pallas_call(
        kernel,
        out_shape=(
            jax.ShapeDtypeStruct((tokens, width), BF16),
            jax.ShapeDtypeStruct((16, features), F32),
        ),
        in_specs=[hbm, hbm, hbm, vmem],
        out_specs=(hbm, vmem),
        scratch_shapes=[
            pltpu.VMEM((tokens, width), BF16),
            pltpu.VMEM((tokens, features), BF16),
            pltpu.VMEM((8, 2 * tokens, 384), BF16),
            pltpu.VMEM((2 * tokens, features), BF16),
            pltpu.VMEM((384, features), F32),
            pltpu.VMEM((RING, RING, 2 * quarter, features), BF16),
            pltpu.VMEM((3, RING, 2 * quarter, features), BF16),
            pltpu.VMEM((RING, 2 * quarter, features), BF16),
            pltpu.VMEM((3, 2 * quarter, features), BF16),
            pltpu.VMEM((2 * quarter + 16, features), F32),
            pltpu.VMEM((DEPTH, 16, features), BF16),
            pltpu.VMEM((DEPTH - 1, 16, features), BF16),
            pltpu.VMEM((width, features), BF16),
            pltpu.VMEM((tokens, width), F32),
            pltpu.VMEM((tokens, 128), F32),
            pltpu.VMEM((tokens, 128), F32),
            pltpu.VMEM((tokens, width), BF16),
            pltpu.SemaphoreType.DMA((11,)),
            pltpu.SemaphoreType.DMA((2, 9)),
            pltpu.SemaphoreType.DMA((2, 3, RING)),
            pltpu.SemaphoreType.DMA((2, 3)),
            pltpu.SemaphoreType.DMA((2, DEPTH - 1)),
            pltpu.SemaphoreType.DMA((2, 1)),
            pltpu.SemaphoreType.DMA((2, 3)),
            pltpu.SemaphoreType.DMA((2, 3)),
            pltpu.SemaphoreType.DMA((2, 3, RING)),
            pltpu.SemaphoreType.DMA((2, 8)),
            pltpu.SemaphoreType.DMA((1,)),
        ],
        compiler_params=pltpu.CompilerParams(
            collective_id=0, has_side_effects=True, vmem_limit_bytes=56 * 2**20
        ),
        name="key_backward",
    )(residual, key_output_gradient, key_projection_matrix, norm_gain_vector.reshape(1, width))
    devices = lax.axis_size("node") * lax.axis_size("group")
    rows = width // devices
    index = lax.axis_index("node") * lax.axis_size("group") + lax.axis_index("group")
    gain = lax.dynamic_slice(norm_gain_vector, (index * rows,), (rows,))
    scale = float(tokens * devices) ** (-0.5)
    weight_grad = sums[:rows] * (gain * scale)[:, None]
    return (residual_gradient, weight_grad)


def solution(mesh):
    return jax.shard_map(
        on_device,
        mesh=mesh,
        in_specs=(P(("node", "group"), None), P(), P("node", None), P(("node", "group"), None)),
        out_specs=(P(("node", "group"), None), P(("node", "group"), None)),
        check_vma=False,
    )
```

time: 522 us -> 75.4 us (0.14)
  waiting for transfers between devices: 336 us -> 0 us
  Pallas kernels: 0 us -> 69.3 us
  starting transfers between devices: 67.3 us -> 0 us
  other arithmetic: 57.6 us -> 2.22 us
  local copies, waits for them, and re-layouts: 31.6 us -> 2.94 us
  matrix products: 14.2 us -> 0 us
  between operations: 14.2 us -> 0.64 us
    all_gather x1 -> x0, waiting for transfers between devices: 308 us -> none  [input_route(): lax.all_gather(key_projection_matrix, 'node', axis=0, tiled=True)]
    pallas_call x0 -> x1, Pallas kernels: none -> 69.3 us  [on_device(): pl.pallas_call(kernel, out_shape=(jax.ShapeDtypeStruct((tokens, width), B...]
    all_to_all x4 -> x0, starting transfers between devices: 67.3 us -> none  [the longest x1 25.7 us: group_section(): lax.all_to_all(scales_two, 'group', split_axis=0, concat_axis=0, tiled=True)]
    unnamed x1 -> x0, other arithmetic: 28.9 us -> none
    all_to_all x4 -> x0, waiting for transfers between devices: 27.6 us -> none  [the longest x1 16.5 us: group_section(): lax.all_to_all(tiles_two, 'group', split_axis=0, concat_axis=0, tiled=True)]
    convert_element_type x6 -> x0, other arithmetic: 22.8 us -> none  [the longest x2 14.3 us: quantize_blocks(): tiles = (blocks / scales.astype(jnp.float32)).astype(jnp.bfloat16)]
    dot_general x2 -> x0, matrix products: 14.2 us -> none  [the longest x1 7.27 us: weight_path(): lax.dot_general(normed_input, key_output_gradient, (((0,), (0,)), ((), ()...]
    reshape x1 -> x0, local copies, waits for them, and re-layouts: 12.2 us -> none  [weight_path(): partial_value.reshape((partial_value.shape[0], width // 128, 128))]
  transfers between devices with their start and end apart: 5 -> 0, of which waited for: 3 -> 0; matrix products, arithmetic and copies ran while one was open for 10% -> 0% of each run, Pallas kernels for 0% -> 0%
where the time goes in v1:
time: 75.4 us; the launch traced here: 75.1 us
  Pallas kernels  69.3 us (92%)
  local copies, waits for them, and re-layouts  2.94 us (4%)
  other arithmetic  2.22 us (3%)
    pallas_call x1, Pallas kernels, on_device(): pl.pallas_call(kernel, out_shape=(jax.ShapeDtypeStruct((tokens, width), B...  69.3 us
    unnamed x1, local copies, waits for them, and re-layouts  2.94 us
    mul x2, other arithmetic, on_device(): weight_grad = sums[:rows] * (gain * scale)[:, None]  2.22 us

profile of v1, /device:TPU:1, one launch (start us, length us, event | category | flops | bytes accessed | tf_op | source)
XLA Modules:
  0.0 75.1 jit_solution(7989030083600598080)
XLA Ops:
  0.6 0.8 %dynamic-slice_multiply_fusion = f32[10]{0:T(128)S(1)} fusion(f32[5120]{0:T(1024)} %param.5, s32[]{:T(128)S(6)} %select_n.3), kind=kLoop, calls=%fused_computation.1 | loop fusion | flops 10 | bytes 84 | tf_op jit(solution)/shard_map/mul | solution.py:416
  1.4 69.3 %key_backward.1 = (bf16[192,5120]{1,0:T(8,128)(2,1)}, f32[16,512]{1,0:T(8,128)}) custom-call(bf16[192,5120]{1,0:T(8,128)(2,1)} %res_hbm.1, bf16[192,512]{1,0:T(8,128)(2,1)} %grad_hbm.1, bf16[320,512]{1,0:T(8,128)(2,1)} %w_hbm.1, f32[1,5120]{1,0:T(1,128)} %bitcast.1), custom_call_target="tpu_custom_call" | custom-call | tf_op jit(solution)/shard_map/key_backward/pallas_call | solution.py:368
  70.7 1.4 %slice_multiply_fusion = f32[10,512]{1,0:T(8,128)} fusion(f32[16,512]{1,0:T(8,128)} %get-tuple-element.5, f32[10]{0:T(128)S(1)} %dynamic-slice_multiply_fusion), kind=kLoop, calls=%fused_computation | loop fusion | flops 5120 | bytes 41000 | tf_op jit(solution)/shard_map/mul | solution.py:416
  72.2 2.9 %copy.7 = bf16[192,5120]{1,0:T(8,128)(2,1)} copy(bf16[192,5120]{1,0:T(8,128)(2,1)} %get-tuple-element.8) | data formatting | bytes 3932160

commit v2 on v1

--- a/solution.py
+++ b/solution.py
@@ -12,6 +12,7 @@
 DEPTH = 16
 Z_LO = 8
 ORDER = (2, 1, 3, 0)
+DIRECT = 128
 
 
 def place():
@@ -52,11 +53,15 @@
     one_sem,
     two_sem,
     three_sem,
+    chain_sem,
     wz_sem,
     wa_sem,
+    wq_sem,
+    wf_sem,
     wb_sem,
     wx_sem,
     wc_sem,
+    wd_sem,
     out_sem,
 ):
     x, y, z, c = place()
@@ -95,7 +100,7 @@
 
     barrier = pltpu.get_barrier_semaphore()
     partners = (
-        [along_z(d) for d in (8, 7, 9, 6, 10, 5, 11, 4, 12, 3, 13, 2, 14, 1, 15)]
+        [along_z(d) for d in (1, 15)]
         + [along_x(d) for d in (1, 2, 3)]
         + [along_y(d) for d in (1, 2, 3)]
         + [other]
@@ -124,52 +129,79 @@
     for b in range(8):
         load_pair[b].start()
     load_w.start()
-    load_grad.wait()
-    load_res.wait()
-
-    def norm(i, carry):
-        at = pl.ds(pl.multiple_of(i * 16, 16), 16)
-        v = res[at].astype(F32)
-        rms = jnp.sqrt(jnp.sum(v * v, axis=1, keepdims=True) / width + 1e-06)
-        rinv = 1.0 / rms
-        rinv_ref[at] = jnp.broadcast_to(rinv, (16, 128))
-        both_grad[pl.ds(pl.multiple_of(c * tokens + i * 16, 16), 16)] = (
-            grad[at].astype(F32) * rinv
-        ).astype(BF16)
-        return carry
-
-    lax.fori_loop(0, tokens // 16, norm, 0)
-
     pl.semaphore_wait(barrier, len(partners))
 
     swap_grad = remote(both_grad.at[mine], both_grad.at[mine], pair_sem, (8,), other)
     swap_res = [
         remote(columns(b, 1 - c), both_res.at[b, mine], pair_sem, (b,), other) for b in range(8)
     ]
-    swap_grad.start()
     for b in range(8):
         swap_res[b].start()
 
-    w_far = remote(
-        w_hbm.at[pl.ds(pl.multiple_of(x * quarter, 16), quarter)],
-        w_rows(y, zh, c, quarter, x * quarter),
-        wz_sem,
-        (0,),
-        along_z(8),
-    )
-    w_far.start()
-    w_near = {d: remote(w_hbm, w_rows(y, zh, c), wa_sem, (d - 1,), along_y(d)) for d in (1, 2, 3)}
-    w_near[1].start()
-    w_near[3].start()
+    fourth = (shard - DIRECT) // RING
+
+    def w_quarter(yy, xx):
+        return w_rows(yy, zh, c, fourth, DIRECT + xx * fourth)
+
+    def w_out(start, count):
+        return w_hbm.at[pl.ds(pl.multiple_of(start, 16), count)]
+
+    def w_near_quarter(d):
+        return remote(
+            w_out(DIRECT + x * fourth, fourth), w_quarter(y, x), wq_sem, (d - 1,), along_y(d)
+        )
+
+    def w_near(d):
+        return remote(
+            w_out(0, DIRECT), w_rows(y, zh, c, DIRECT), wa_sem, (d - 1,), along_y(d)
+        )
+
+    def w_fan(d, e):
+        piece = w_quarter((y + RING - d) % RING, x)
+        return remote(piece, piece, wf_sem, (e - 1, d - 1), along_x(e))
+
+    for d in (2, 1, 3):
+        w_near_quarter(d).start()
+    for d in (2, 1, 3):
+        w_near(d).start()
+
+    def tell(k):
+        for d in (1 << k, DEPTH - (1 << k)):
+            pl.semaphore_signal(chain_sem.at[k], inc=1, device_id=along_z(d), device_id_type=MESH)
+
+    def hear(k):
+        pl.semaphore_wait(chain_sem.at[k], 2)
+
+    tell(0)
+    load_grad.wait()
+    load_res.wait()
+
+    def square(i, total):
+        for k in range(4):
+            v = res[:, pl.ds(pl.multiple_of(i * 512 + k * 128, 128), 128)].astype(F32)
+            total = total + v * v
+        return total
+
+    squares = lax.fori_loop(0, width // 512, square, jnp.zeros((tokens, 128), F32))
+    rinv = 1.0 / jnp.sqrt(jnp.sum(squares, axis=1, keepdims=True) / width + 1e-06)
+    rinv_ref[...] = jnp.broadcast_to(rinv, (tokens, 128))
+    both_grad[mine] = (grad[...].astype(F32) * rinv).astype(BF16)
+
+    swap_grad.start()
     load_w.wait()
 
-    def to_other(yy, hi):
-        return remote(
-            w_rows(yy, hi, c), w_rows(yy, hi, c), wc_sem, (yy * 2 + hi,), other
-        )
-
-    to_other(y, zh).start()
-
+    def to_other(yy):
+        return remote(w_rows(yy, zh, c), w_rows(yy, zh, c), wc_sem, (yy,), other)
+
+    to_other(y).start()
+
+    for d in (1, 3, 2):
+        w_near_quarter(d).wait_recv()
+        for e in (2, 1, 3):
+            w_fan(d, e).start()
+
+    hear(0)
+    tell(1)
     for b in range(8):
         load_pair[b].wait()
     swap_grad.wait_recv()
@@ -201,6 +233,9 @@
     for step in ORDER:
         yy = (y + step) % RING
         partial_block(yy)
+        if step == 3:
+            hear(1)
+            tell(2)
 
         @pl.when(c == 0)
         def _(yy=yy):
@@ -213,15 +248,19 @@
             for d in (2, 1, 3):
                 copy_one(d, (x + step) % RING).start()
 
-    w_far.wait_recv()
+    w_far = remote(
+        w_out(x * quarter, quarter), w_rows(y, zh, c, quarter, x * quarter), wz_sem, (0,), along_z(8)
+    )
+    hear(2)
+    w_far.start()
+
     lo = 1 - zh
 
+    def w_piece(core, yy, xx):
+        return w_rows(yy, lo, core, quarter, xx * quarter)
+
     def w_side(d):
-        piece = w_rows(y, lo, c, quarter, x * quarter)
-        return remote(piece, piece, wb_sem, (d - 1,), along_y(d))
-
-    for d in (2, 1, 3):
-        w_side(d).start()
+        return remote(w_piece(c, y, x), w_piece(c, y, x), wb_sem, (d - 1,), along_second(d))
 
     def copy_two(e):
         return remote(red.at[(second + e) % RING], recv2.at[e - 1], two_sem, (e - 1,), along_second(e))
@@ -246,16 +285,21 @@
         if step:
             copy_two(step).start()
 
-    def w_across(d, yy):
-        piece = w_rows(yy, lo, c, quarter, x * quarter)
-        return remote(piece, piece, wx_sem, (d - 1, yy), along_x(d))
-
-    for d in (1, 2, 3):
-        w_side(d).wait_recv()
-    for yy in range(RING):
-        for d in (2, 1, 3):
-            w_across(d, yy).start()
-    w_near[2].start()
+    def piece_of(k, back=0):
+        xx, yy = (x + RING - back) % RING, (y + RING - back) % RING
+        return k + c * (yy - k), xx + c * (k - xx)
+
+    def w_across(d, k):
+        piece = w_piece(c, *piece_of(k))
+        return remote(piece, piece, wx_sem, (d - 1, k), along_first(d))
+
+    def w_far_other(yy, xx):
+        piece = w_piece(c, yy, xx)
+        return remote(piece, piece, wd_sem, (yy, xx), other)
+
+    w_far.wait_recv()
+    for d in (2, 1, 3):
+        w_side(d).start()
 
     dot_ref[...] = jnp.zeros_like(dot_ref)
 
@@ -269,19 +313,25 @@
         )
         value = value * gain_ref[:, at]
         scaled[:, at] = value
-        dot_ref[...] += jnp.sum(value * res[:, at].astype(F32), axis=1, keepdims=True)
-
-    def from_other(yy, hi):
-        remote(
-            w_rows(yy, hi, 1 - c), w_rows(yy, hi, 1 - c), wc_sem, (yy * 2 + hi,), other
-        ).wait_recv()
-
-    for d in (1, 3):
-        w_near[d].wait_recv()
-        to_other((y + RING - d) % RING, zh).start()
-    for d in (0, 1, 3):
+        value = value * res[:, at].astype(F32)
+        part = dot_ref[...]
+        for k in range(2 * shard // 128):
+            part = part + value[:, k * 128 : (k + 1) * 128]
+        dot_ref[...] = part
+
+    def from_other(yy):
+        piece = w_rows(yy, zh, 1 - c)
+        remote(piece, piece, wc_sem, (yy,), other).wait_recv()
+
+    for d in (1, 3, 2):
+        w_near(d).wait_recv()
+        for e in (1, 2, 3):
+            piece = w_quarter((y + RING - d) % RING, (x + RING - e) % RING)
+            remote(piece, piece, wf_sem, (e - 1, d - 1), along_x(e)).wait_recv()
+        to_other((y + RING - d) % RING).start()
+    for d in (0, 1, 3, 2):
         yy = (y + RING - d) % RING
-        from_other(yy, zh)
+        from_other(yy)
         features(yy * 2 + zh)
 
     for e in (1, 3, 2):
@@ -307,55 +357,76 @@
     for d in distances:
         copy_three(d).start()
 
-    w_near[2].wait_recv()
-    to_other((y + 2) % RING, zh).start()
-    from_other((y + 2) % RING, zh)
-    features((y + 2) % RING * 2 + zh)
-
+    for d in (1, 2, 3):
+        w_side(d).wait_recv()
+    for k in range(RING):
+        for d in (2, 1, 3):
+            w_across(d, k).start()
+    for k in range(RING):
+        w_far_other(*piece_of(k)).start()
+
+    for k in range(RING):
+        for d in (1, 3, 2):
+            piece = w_piece(c, *piece_of(k, d))
+            remote(piece, piece, wx_sem, (d - 1, k), along_first(d)).wait_recv()
+            w_far_other(*piece_of(k, d)).start()
     for yy in range(RING):
-        for d in (1, 2, 3):
-            w_across_in = w_rows(yy, lo, c, quarter, (x + RING - d) % RING * quarter)
-            remote(w_across_in, w_across_in, wx_sem, (d - 1, yy), along_x(d)).wait_recv()
-        to_other(yy, lo).start()
-    for yy in range(RING):
-        from_other(yy, lo)
+        for xx in range(RING):
+            piece = w_piece(1 - c, yy, xx)
+            remote(piece, piece, wd_sem, (yy, xx), other).wait_recv()
         features(yy * 2 + lo)
 
     def finish(i, carry):
         at = pl.ds(pl.multiple_of(i * 16, 16), 16)
         rinv = rinv_ref[at][:, :1]
-        factor = dot_ref[at][:, :1] * (1.0 / width) * rinv * rinv
+        factor = jnp.sum(dot_ref[at], axis=1, keepdims=True) * (1.0 / width) * rinv * rinv
         out[at] = ((scaled[at] - res[at].astype(F32) * factor) * rinv).astype(BF16)
         return carry
 
-    lax.fori_loop(0, tokens // 16, finish, 0)
-    store = pltpu.make_async_copy(out, out_hbm, out_sem.at[0])
-    store.start()
+    stores = []
+    for k in range(4):
+        part = pl.ds(k * (tokens // 4), tokens // 4)
+        lax.fori_loop(k * (tokens // 64), (k + 1) * (tokens // 64), finish, 0)
+        stores.append(pltpu.make_async_copy(out.at[part], out_hbm.at[part], out_sem.at[k]))
+        stores[-1].start()
+
+    place_of_rows = (lax.axis_index("node") * (RING * Z_LO) + lax.axis_index("group")) * rows
+    lane = lax.broadcasted_iota(jnp.int32, (16, width), 1)
+    row = lax.broadcasted_iota(jnp.int32, (16, width), 0)
+    own_gain = jnp.sum(
+        jnp.where(lane == row + place_of_rows, gain_ref[...], 0.0), axis=1, keepdims=True
+    )
+    scale = float(tokens * RING * RING * DEPTH * 2) ** (-0.5)
 
     for d in distances:
         copy_three(d).wait_recv()
     total = send3[z].astype(F32)
     for k in range(DEPTH - 1):
         total = total + recv3[k].astype(F32)
-    wg_ref[...] = total
+    wg_ref[...] = (total * (own_gain * scale))[:rows]
 
     swap_grad.wait_send()
     for b in range(8):
         swap_res[b].wait_send()
     w_far.wait_send()
     for d in (1, 2, 3):
-        w_near[d].wait_send()
+        w_near(d).wait_send()
+        w_near_quarter(d).wait_send()
         w_side(d).wait_send()
         copy_two(d).wait_send()
+        for e in (1, 2, 3):
+            w_fan(d, e).wait_send()
         for s in range(RING):
             copy_one(d, s).wait_send()
             w_across(d, s).wait_send()
     for yy in range(RING):
-        for hi in range(2):
-            to_other(yy, hi).wait_send()
+        to_other(yy).wait_send()
+        for d in range(RING):
+            w_far_other(*piece_of(yy, d)).wait_send()
     for d in distances:
         copy_three(d).wait_send()
-    store.wait()
+    for store in stores:
+        store.wait()
 
 
 def on_device(residual, norm_gain_vector, key_projection_matrix, key_output_gradient):
@@ -363,16 +434,16 @@
     features = key_output_gradient.shape[1]
     shard = key_projection_matrix.shape[0]
     quarter = shard // RING
-    hbm = pl.BlockSpec(memory_space=pl.ANY)
+    hbm = pl.BlockSpec(memory_space=pltpu.HBM)
     vmem = pl.BlockSpec(memory_space=pltpu.VMEM)
-    residual_gradient, sums = pl.pallas_call(
+    return pl.pallas_call(
         kernel,
         out_shape=(
-            jax.ShapeDtypeStruct((tokens, width), BF16),
-            jax.ShapeDtypeStruct((16, features), F32),
+            pltpu.VMEM((tokens, width), BF16),
+            pltpu.VMEM((shard // (RING * Z_LO), features), F32),
         ),
         in_specs=[hbm, hbm, hbm, vmem],
-        out_specs=(hbm, vmem),
+        out_specs=(pl.BlockSpec(memory_space=pl.ANY), vmem),
         scratch_shapes=[
             pltpu.VMEM((tokens, width), BF16),
             pltpu.VMEM((tokens, features), BF16),
@@ -396,25 +467,22 @@
             pltpu.SemaphoreType.DMA((2, 3, RING)),
             pltpu.SemaphoreType.DMA((2, 3)),
             pltpu.SemaphoreType.DMA((2, DEPTH - 1)),
+            pltpu.SemaphoreType.REGULAR((3,)),
             pltpu.SemaphoreType.DMA((2, 1)),
             pltpu.SemaphoreType.DMA((2, 3)),
             pltpu.SemaphoreType.DMA((2, 3)),
+            pltpu.SemaphoreType.DMA((2, 3, 3)),
+            pltpu.SemaphoreType.DMA((2, 3)),
             pltpu.SemaphoreType.DMA((2, 3, RING)),
-            pltpu.SemaphoreType.DMA((2, 8)),
-            pltpu.SemaphoreType.DMA((1,)),
+            pltpu.SemaphoreType.DMA((2, RING)),
+            pltpu.SemaphoreType.DMA((2, RING, RING)),
+            pltpu.SemaphoreType.DMA((4,)),
         ],
         compiler_params=pltpu.CompilerParams(
-            collective_id=0, has_side_effects=True, vmem_limit_bytes=56 * 2**20
+            collective_id=0, has_side_effects=True, vmem_limit_bytes=54 * 2**20
         ),
         name="key_backward",
     )(residual, key_output_gradient, key_projection_matrix, norm_gain_vector.reshape(1, width))
-    devices = lax.axis_size("node") * lax.axis_size("group")
-    rows = width // devices
-    index = lax.axis_index("node") * lax.axis_size("group") + lax.axis_index("group")
-    gain = lax.dynamic_slice(norm_gain_vector, (index * rows,), (rows,))
-    scale = float(tokens * devices) ** (-0.5)
-    weight_grad = sums[:rows] * (gain * scale)[:, None]
-    return (residual_gradient, weight_grad)
 
 
 def solution(mesh):

time: 75.4 us -> 70.6 us (0.936)
  other arithmetic: 2.22 us -> 0 us
  Pallas kernels: 69.3 us -> 67.9 us
  local copies, waits for them, and re-layouts: 2.94 us -> 1.89 us
    mul x2 -> x0, other arithmetic: 2.22 us -> none  [on_device(): weight_grad = sums[:rows] * (gain * scale)[:, None]]
    pallas_call x1, Pallas kernels: 69.3 us -> 67.9 us  [on_device(): pl.pallas_call(kernel, out_shape=(pltpu.VMEM((tokens, width), BF16), pltp...]
    unnamed x1 -> x2, local copies, waits for them, and re-layouts: 2.94 us -> 1.89 us
where the time goes in v2:
time: 70.6 us; the launch traced here: 70.4 us
  Pallas kernels  67.9 us (96%)
  local copies, waits for them, and re-layouts  1.89 us (3%)
    pallas_call x1, Pallas kernels, on_device(): pl.pallas_call(kernel, out_shape=(pltpu.VMEM((tokens, width), BF16), pltp...  67.9 us
    unnamed x2, local copies, waits for them, and re-layouts  1.89 us

profile of v2, /device:TPU:1, one launch (start us, length us, event | category | flops | bytes accessed | tf_op | source)
XLA Modules:
  0.0 70.4 jit_solution(16631571078975680070)
XLA Ops:
  0.6 67.9 %key_backward.1 = (bf16[192,5120]{1,0:T(8,128)(2,1)S(1)}, f32[10,512]{1,0:T(8,128)S(1)}) custom-call(bf16[192,5120]{1,0:T(8,128)(2,1)} %res_hbm.1, bf16[192,512]{1,0:T(8,128)(2,1)} %grad_hbm.1, bf16[320,512]{1,0:T(8,128)(2,1)} %w_hbm.1, f32[1,5120]{1,0:T(1,128)} %bitcast.1), custom_call_target="tpu_custom_call" | custom-call | tf_op jit(solution)/shard_map/key_backward/pallas_call | solution.py:439
  68.5 1.3 %copy.8 = bf16[192,5120]{1,0:T(8,128)(2,1)} copy(bf16[192,5120]{1,0:T(8,128)(2,1)S(1)} %get-tuple-element.2) | data formatting | bytes 3932160
  69.8 0.6 copy.9

commit v3 on v2

--- a/solution.py
+++ b/solution.py
@@ -12,7 +12,7 @@
 DEPTH = 16
 Z_LO = 8
 ORDER = (2, 1, 3, 0)
-DIRECT = 128
+REACH = 4
 
 
 def place():
@@ -56,8 +56,7 @@
     chain_sem,
     wz_sem,
     wa_sem,
-    wq_sem,
-    wf_sem,
+    ws_sem,
     wb_sem,
     wx_sem,
     wc_sem,
@@ -138,30 +137,25 @@
     for b in range(8):
         swap_res[b].start()
 
-    fourth = (shard - DIRECT) // RING
-
-    def w_quarter(yy, xx):
-        return w_rows(yy, zh, c, fourth, DIRECT + xx * fourth)
+    half_shard = shard // 2
+    parity = z % 2
 
     def w_out(start, count):
         return w_hbm.at[pl.ds(pl.multiple_of(start, 16), count)]
 
-    def w_near_quarter(d):
-        return remote(
-            w_out(DIRECT + x * fourth, fourth), w_quarter(y, x), wq_sem, (d - 1,), along_y(d)
-        )
-
     def w_near(d):
         return remote(
-            w_out(0, DIRECT), w_rows(y, zh, c, DIRECT), wa_sem, (d - 1,), along_y(d)
+            w_out(parity * half_shard, half_shard),
+            w_rows(y, zh, c, half_shard, parity * half_shard),
+            wa_sem,
+            (d - 1,),
+            along_y(d),
         )
 
-    def w_fan(d, e):
-        piece = w_quarter((y + RING - d) % RING, x)
-        return remote(piece, piece, wf_sem, (e - 1, d - 1), along_x(e))
-
-    for d in (2, 1, 3):
-        w_near_quarter(d).start()
+    def w_swap(d):
+        piece = w_rows((y + RING - d) % RING, zh, c, half_shard, parity * half_shard)
+        return remote(piece, piece, ws_sem, (d - 1,), device(x, y, z + 1 - 2 * parity, c))
+
     for d in (2, 1, 3):
         w_near(d).start()
 
@@ -194,11 +188,6 @@
         return remote(w_rows(yy, zh, c), w_rows(yy, zh, c), wc_sem, (yy,), other)
 
     to_other(y).start()
-
-    for d in (1, 3, 2):
-        w_near_quarter(d).wait_recv()
-        for e in (2, 1, 3):
-            w_fan(d, e).start()
 
     hear(0)
     tell(1)
@@ -230,12 +219,31 @@
 
         lax.fori_loop(0, 2, half, 0)
 
+    z_lo = z % Z_LO
+    sends_far = (z_lo == 0) | (z_lo == Z_LO - 1)
+
+    def w_far(j):
+        target = (z + DEPTH + jnp.where(z_lo == 0, -1 - j, 1 + j)) % DEPTH
+        return pltpu.make_async_remote_copy(
+            src_ref=w_out(x * quarter, quarter),
+            dst_ref=w_rows(y, zh, c, quarter, x * quarter),
+            send_sem=wz_sem.at[0, j],
+            recv_sem=wz_sem.at[1, 0],
+            device_id=device(x, y, target, c),
+            device_id_type=MESH,
+        )
+
     for step in ORDER:
         yy = (y + step) % RING
         partial_block(yy)
-        if step == 3:
+        if step == 1:
             hear(1)
             tell(2)
+
+            @pl.when(sends_far)
+            def _():
+                for j in range(REACH - 1, -1, -1):
+                    w_far(j).start()
 
         @pl.when(c == 0)
         def _(yy=yy):
@@ -248,11 +256,9 @@
             for d in (2, 1, 3):
                 copy_one(d, (x + step) % RING).start()
 
-    w_far = remote(
-        w_out(x * quarter, quarter), w_rows(y, zh, c, quarter, x * quarter), wz_sem, (0,), along_z(8)
-    )
-    hear(2)
-    w_far.start()
+    for d in (1, 3, 2):
+        w_near(d).wait_recv()
+        w_swap(d).start()
 
     lo = 1 - zh
 
@@ -284,22 +290,38 @@
         lax.fori_loop(0, 2 * quarter // 16, add, 0)
         if step:
             copy_two(step).start()
-
-    def piece_of(k, back=0):
-        xx, yy = (x + RING - back) % RING, (y + RING - back) % RING
-        return k + c * (yy - k), xx + c * (k - xx)
-
-    def w_across(d, k):
-        piece = w_piece(c, *piece_of(k))
-        return remote(piece, piece, wx_sem, (d - 1, k), along_first(d))
-
-    def w_far_other(yy, xx):
-        piece = w_piece(c, yy, xx)
-        return remote(piece, piece, wd_sem, (yy, xx), other)
-
-    w_far.wait_recv()
-    for d in (2, 1, 3):
-        w_side(d).start()
+        if step == 1:
+            w_far(0).wait_recv()
+            for d in (2, 1, 3):
+                w_side(d).start()
+
+    def w_across(d, yy):
+        piece = w_piece(0, yy, x)
+        return remote(piece, piece, wx_sem, (d - 1, yy), along_x(d))
+
+    def w_whole(d):
+        piece = w_rows(y, lo, 1)
+        return remote(piece, piece, wx_sem, (d - 1, 0), along_y(d))
+
+    def to_other_far(yy):
+        return remote(w_rows(yy, lo, c), w_rows(yy, lo, c), wd_sem, (yy,), other)
+
+    for d in (1, 3, 2):
+        w_swap(d).wait_recv()
+        to_other((y + RING - d) % RING).start()
+    for d in (1, 2, 3):
+        w_side(d).wait_recv()
+
+    @pl.when(c == 0)
+    def _():
+        for back in (0, 1, 3, 2):
+            for d in (2, 1, 3):
+                w_across(d, (y + RING - back) % RING).start()
+
+    @pl.when(c == 1)
+    def _():
+        for d in (1, 3, 2):
+            w_whole(d).start()
 
     dot_ref[...] = jnp.zeros_like(dot_ref)
 
@@ -323,12 +345,6 @@
         piece = w_rows(yy, zh, 1 - c)
         remote(piece, piece, wc_sem, (yy,), other).wait_recv()
 
-    for d in (1, 3, 2):
-        w_near(d).wait_recv()
-        for e in (1, 2, 3):
-            piece = w_quarter((y + RING - d) % RING, (x + RING - e) % RING)
-            remote(piece, piece, wf_sem, (e - 1, d - 1), along_x(e)).wait_recv()
-        to_other((y + RING - d) % RING).start()
     for d in (0, 1, 3, 2):
         yy = (y + RING - d) % RING
         from_other(yy)
@@ -353,28 +369,38 @@
     def copy_three(d):
         return remote(send3.at[(z + d) % DEPTH], recv3.at[d - 1], three_sem, (d - 1,), along_z(d))
 
+    hear(2)
     distances = (8, 7, 9, 6, 10, 5, 11, 4, 12, 3, 13, 2, 14, 1, 15)
     for d in distances:
         copy_three(d).start()
 
-    for d in (1, 2, 3):
-        w_side(d).wait_recv()
-    for k in range(RING):
-        for d in (2, 1, 3):
-            w_across(d, k).start()
-    for k in range(RING):
-        w_far_other(*piece_of(k)).start()
-
-    for k in range(RING):
-        for d in (1, 3, 2):
-            piece = w_piece(c, *piece_of(k, d))
-            remote(piece, piece, wx_sem, (d - 1, k), along_first(d)).wait_recv()
-            w_far_other(*piece_of(k, d)).start()
-    for yy in range(RING):
-        for xx in range(RING):
-            piece = w_piece(1 - c, yy, xx)
-            remote(piece, piece, wd_sem, (yy, xx), other).wait_recv()
+    def from_other_far(yy):
+        piece = w_rows(yy, lo, 1 - c)
+        remote(piece, piece, wd_sem, (yy,), other).wait_recv()
         features(yy * 2 + lo)
+
+    before = None
+    for back in (0, 1, 3, 2):
+        yy = (y + RING - back) % RING
+
+        @pl.when(c == 0)
+        def _(yy=yy):
+            for d in (1, 3, 2):
+                piece = w_piece(0, yy, (x + RING - d) % RING)
+                remote(piece, piece, wx_sem, (d - 1, yy), along_x(d)).wait_recv()
+
+        if back:
+
+            @pl.when(c == 1)
+            def _(yy=yy, back=back):
+                piece = w_rows(yy, lo, 1)
+                remote(piece, piece, wx_sem, (back - 1, 0), along_y(back)).wait_recv()
+
+        to_other_far(yy).start()
+        if before is not None:
+            from_other_far(before)
+        before = yy
+    from_other_far(before)
 
     def finish(i, carry):
         at = pl.ds(pl.multiple_of(i * 16, 16), 16)
@@ -408,21 +434,33 @@
     swap_grad.wait_send()
     for b in range(8):
         swap_res[b].wait_send()
-    w_far.wait_send()
+    @pl.when(sends_far)
+    def _():
+        for j in range(REACH):
+            w_far(j).wait_send()
+
     for d in (1, 2, 3):
         w_near(d).wait_send()
-        w_near_quarter(d).wait_send()
+        w_swap(d).wait_send()
         w_side(d).wait_send()
         copy_two(d).wait_send()
-        for e in (1, 2, 3):
-            w_fan(d, e).wait_send()
         for s in range(RING):
             copy_one(d, s).wait_send()
-            w_across(d, s).wait_send()
+
+    @pl.when(c == 0)
+    def _():
+        for d in (1, 2, 3):
+            for yy in range(RING):
+                w_across(d, yy).wait_send()
+
+    @pl.when(c == 1)
+    def _():
+        for d in (1, 2, 3):
+            w_whole(d).wait_send()
+
     for yy in range(RING):
         to_other(yy).wait_send()
-        for d in range(RING):
-            w_far_other(*piece_of(yy, d)).wait_send()
+        to_other_far(yy).wait_send()
     for d in distances:
         copy_three(d).wait_send()
     for store in stores:
@@ -468,14 +506,13 @@
             pltpu.SemaphoreType.DMA((2, 3)),
             pltpu.SemaphoreType.DMA((2, DEPTH - 1)),
             pltpu.SemaphoreType.REGULAR((3,)),
-            pltpu.SemaphoreType.DMA((2, 1)),
+            pltpu.SemaphoreType.DMA((2, REACH)),
             pltpu.SemaphoreType.DMA((2, 3)),
             pltpu.SemaphoreType.DMA((2, 3)),
-            pltpu.SemaphoreType.DMA((2, 3, 3)),
             pltpu.SemaphoreType.DMA((2, 3)),
             pltpu.SemaphoreType.DMA((2, 3, RING)),
             pltpu.SemaphoreType.DMA((2, RING)),
-            pltpu.SemaphoreType.DMA((2, RING, RING)),
+            pltpu.SemaphoreType.DMA((2, RING)),
             pltpu.SemaphoreType.DMA((4,)),
         ],
         compiler_params=pltpu.CompilerParams(

time: 70.6 us -> 63.6 us (0.901)
  Pallas kernels: 67.9 us -> 60.3 us
    pallas_call x1, Pallas kernels: 67.9 us -> 60.3 us  [on_device(): pl.pallas_call(kernel, out_shape=(pltpu.VMEM((tokens, width), BF16), pltp...]
where the time goes in v3:
time: 63.6 us; the launch traced here: 62.8 us
  Pallas kernels  60.3 us (95%)
  local copies, waits for them, and re-layouts  1.89 us (3%)
  between operations  0.64 us (1%)
    pallas_call x1, Pallas kernels, on_device(): pl.pallas_call(kernel, out_shape=(pltpu.VMEM((tokens, width), BF16), pltp...  60.3 us
    unnamed x2, local copies, waits for them, and re-layouts  1.89 us

profile of v3, /device:TPU:1, one launch (start us, length us, event | category | flops | bytes accessed | tf_op | source)
XLA Modules:
  0.0 62.8 jit_solution(12479991840472707325)
XLA Ops:
  0.6 60.3 %key_backward.1 = (bf16[192,5120]{1,0:T(8,128)(2,1)S(1)}, f32[10,512]{1,0:T(8,128)S(1)}) custom-call(bf16[192,5120]{1,0:T(8,128)(2,1)} %res_hbm.1, bf16[192,512]{1,0:T(8,128)(2,1)} %grad_hbm.1, bf16[320,512]{1,0:T(8,128)(2,1)} %w_hbm.1, f32[1,5120]{1,0:T(1,128)} %bitcast.1), custom_call_target="tpu_custom_call" | custom-call | tf_op jit(solution)/shard_map/key_backward/pallas_call | solution.py:477
  60.9 1.3 %copy.8 = bf16[192,5120]{1,0:T(8,128)(2,1)} copy(bf16[192,5120]{1,0:T(8,128)(2,1)S(1)} %get-tuple-element.2) | data formatting | bytes 3932160
  62.2 0.6 copy.9

commit v4 on v3

--- a/solution.py
+++ b/solution.py
@@ -11,6 +11,7 @@
 RING = 4
 DEPTH = 16
 Z_LO = 8
+BLOCK = 128
 ORDER = (2, 1, 3, 0)
 REACH = 4
 
@@ -29,25 +30,25 @@
     grad_hbm,
     w_hbm,
     gain_ref,
-    out_hbm,
+    out,
     wg_ref,
     res,
     grad,
     both_res,
     both_grad,
-    product,
+    turned,
     send1,
     recv1,
     red,
     recv2,
     acc,
+    packed,
     send3,
     recv3,
     w,
     scaled,
     rinv_ref,
     dot_ref,
-    out,
     local_sem,
     pair_sem,
     one_sem,
@@ -61,7 +62,6 @@
     wx_sem,
     wc_sem,
     wd_sem,
-    out_sem,
 ):
     x, y, z, c = place()
     zh = z // Z_LO
@@ -119,23 +119,24 @@
     load_res = pltpu.make_async_copy(res_hbm, res, local_sem.at[0])
     load_grad = pltpu.make_async_copy(grad_hbm, grad, local_sem.at[1])
     load_w = pltpu.make_async_copy(w_hbm, w_rows(y, zh, c), local_sem.at[2])
-    load_pair = [
-        pltpu.make_async_copy(columns(b, c), both_res.at[b, mine], local_sem.at[3 + b])
-        for b in range(8)
-    ]
+
+    def load_pair(b):
+        return pltpu.make_async_copy(columns(b, c), both_res.at[b, mine], local_sem.at[3 + b])
+
     load_res.start()
     load_grad.start()
     for b in range(8):
-        load_pair[b].start()
+        load_pair(b).start()
     load_w.start()
     pl.semaphore_wait(barrier, len(partners))
 
     swap_grad = remote(both_grad.at[mine], both_grad.at[mine], pair_sem, (8,), other)
-    swap_res = [
-        remote(columns(b, 1 - c), both_res.at[b, mine], pair_sem, (b,), other) for b in range(8)
-    ]
+
+    def swap_res(b):
+        return remote(columns(b, 1 - c), both_res.at[b, mine], pair_sem, (b,), other)
+
     for b in range(8):
-        swap_res[b].start()
+        swap_res(b).start()
 
     half_shard = shard // 2
     parity = z % 2
@@ -169,6 +170,8 @@
     tell(0)
     load_grad.wait()
     load_res.wait()
+    hear(0)
+    tell(1)
 
     def square(i, total):
         for k in range(4):
@@ -188,36 +191,6 @@
         return remote(w_rows(yy, zh, c), w_rows(yy, zh, c), wc_sem, (yy,), other)
 
     to_other(y).start()
-
-    hear(0)
-    tell(1)
-    for b in range(8):
-        load_pair[b].wait()
-    swap_grad.wait_recv()
-    for b in range(8):
-        swap_res[b].wait_recv()
-
-    def copy_one(d, s):
-        return remote(
-            send1.at[(first + d) % RING, s], recv1.at[d - 1, s], one_sem, (d - 1, s), along_first(d)
-        )
-
-    def partial_block(yy):
-        def half(hi, carry):
-            product[...] = lax.dot_general(
-                both_res[yy * 2 + hi],
-                both_grad[...],
-                (((0,), (0,)), ((), ())),
-                preferred_element_type=F32,
-            )
-            for q in range(RING):
-                at = pl.ds(pl.multiple_of(c * 64 + q * quarter, 16), quarter)
-                send1[
-                    q + c * (yy - q), yy + c * (q - yy), pl.ds(pl.multiple_of(hi * quarter, 16), quarter)
-                ] = product[at].astype(BF16)
-            return carry
-
-        lax.fori_loop(0, 2, half, 0)
 
     z_lo = z % Z_LO
     sends_far = (z_lo == 0) | (z_lo == Z_LO - 1)
@@ -233,17 +206,47 @@
             device_id_type=MESH,
         )
 
+    hear(1)
+
+    @pl.when(sends_far)
+    def _():
+        for j in range(REACH - 1, -1, -1):
+            w_far(j).start()
+
+    tell(2)
+
+    def turn(b, carry):
+        load_pair(b).wait()
+        swap_res(b).wait_recv()
+        turned[b] = both_res[b].T
+        return carry
+
+    lax.fori_loop(0, 8, turn, 0)
+    swap_grad.wait_recv()
+
+    def copy_one(d, s):
+        return remote(
+            send1.at[(first + d) % RING, s], recv1.at[d - 1, s], one_sem, (d - 1, s), along_first(d)
+        )
+
+    def partial_block(yy):
+        def half(hi, carry):
+            value = jnp.dot(
+                turned[yy * 2 + hi, pl.ds(pl.multiple_of(c * 64, 64), shard)],
+                both_grad[...],
+                preferred_element_type=F32,
+            ).astype(BF16)
+            for q in range(RING):
+                send1[
+                    q + c * (yy - q), yy + c * (q - yy), pl.ds(pl.multiple_of(hi * quarter, 16), quarter)
+                ] = value[q * quarter : (q + 1) * quarter]
+            return carry
+
+        lax.fori_loop(0, 2, half, 0)
+
     for step in ORDER:
         yy = (y + step) % RING
         partial_block(yy)
-        if step == 1:
-            hear(1)
-            tell(2)
-
-            @pl.when(sends_far)
-            def _():
-                for j in range(REACH - 1, -1, -1):
-                    w_far(j).start()
 
         @pl.when(c == 0)
         def _(yy=yy):
@@ -270,6 +273,37 @@
 
     def copy_two(e):
         return remote(red.at[(second + e) % RING], recv2.at[e - 1], two_sem, (e - 1,), along_second(e))
+
+    def w_across(d, yy):
+        piece = w_piece(0, yy, x)
+        return remote(piece, piece, wx_sem, (d - 1, yy), along_x(d))
+
+    def w_whole(d):
+        piece = w_rows(y, lo, 1)
+        return remote(piece, piece, wx_sem, (d - 1, 0), along_y(d))
+
+    def to_other_far(yy):
+        return remote(w_rows(yy, lo, c), w_rows(yy, lo, c), wd_sem, (yy,), other)
+
+    def first_part():
+        w_far(0).wait_recv()
+        for d in (2, 1, 3):
+            w_side(d).start()
+
+    def second_part():
+        for d in (1, 2, 3):
+            w_side(d).wait_recv()
+
+        @pl.when(c == 0)
+        def _():
+            for back in (0, 1, 3, 2):
+                for d in (2, 1, 3):
+                    w_across(d, (y + RING - back) % RING).start()
+
+        @pl.when(c == 1)
+        def _():
+            for d in (1, 3, 2):
+                w_whole(d).start()
 
     for step in ORDER:
         s = (second + step) % RING
@@ -291,39 +325,15 @@
         if step:
             copy_two(step).start()
         if step == 1:
-            w_far(0).wait_recv()
-            for d in (2, 1, 3):
-                w_side(d).start()
-
-    def w_across(d, yy):
-        piece = w_piece(0, yy, x)
-        return remote(piece, piece, wx_sem, (d - 1, yy), along_x(d))
-
-    def w_whole(d):
-        piece = w_rows(y, lo, 1)
-        return remote(piece, piece, wx_sem, (d - 1, 0), along_y(d))
-
-    def to_other_far(yy):
-        return remote(w_rows(yy, lo, c), w_rows(yy, lo, c), wd_sem, (yy,), other)
+            first_part()
+        if step == 3:
+            second_part()
 
     for d in (1, 3, 2):
         w_swap(d).wait_recv()
         to_other((y + RING - d) % RING).start()
-    for d in (1, 2, 3):
-        w_side(d).wait_recv()
-
-    @pl.when(c == 0)
-    def _():
-        for back in (0, 1, 3, 2):
-            for d in (2, 1, 3):
-                w_across(d, (y + RING - back) % RING).start()
-
-    @pl.when(c == 1)
-    def _():
-        for d in (1, 3, 2):
-            w_whole(d).start()
-
     dot_ref[...] = jnp.zeros_like(dot_ref)
+    packed[...] = jnp.zeros_like(packed)
 
     def features(block):
         at = pl.ds(pl.multiple_of(block * (2 * shard), 128), 2 * shard)
@@ -345,11 +355,6 @@
         piece = w_rows(yy, zh, 1 - c)
         remote(piece, piece, wc_sem, (yy,), other).wait_recv()
 
-    for d in (0, 1, 3, 2):
-        yy = (y + RING - d) % RING
-        from_other(yy)
-        features(yy * 2 + zh)
-
     for e in (1, 3, 2):
         copy_two(e).wait_recv()
 
@@ -362,9 +367,14 @@
         return carry
 
     lax.fori_loop(0, 2 * quarter // 16, add_two, 0)
-    acc[2 * quarter :] = jnp.zeros((acc.shape[0] - 2 * quarter, acc.shape[1]), F32)
+    high, wide = 16 - rows, acc.shape[1] - BLOCK
     for k in range(DEPTH):
-        send3[k] = acc[k * rows : k * rows + 16].astype(BF16)
+        at = k * rows
+        packed[k, :rows] = acc[at : at + rows, :wide]
+        packed[k, rows:, :BLOCK] = acc[at : at + high, wide:]
+        packed[k, rows : 2 * rows - high, BLOCK : 2 * BLOCK] = acc[at + high : at + rows, wide:]
+    for k in range(DEPTH):
+        send3[k] = packed[k].astype(BF16)
 
     def copy_three(d):
         return remote(send3.at[(z + d) % DEPTH], recv3.at[d - 1], three_sem, (d - 1,), along_z(d))
@@ -373,6 +383,11 @@
     distances = (8, 7, 9, 6, 10, 5, 11, 4, 12, 3, 13, 2, 14, 1, 15)
     for d in distances:
         copy_three(d).start()
+
+    for d in (0, 1, 3, 2):
+        yy = (y + RING - d) % RING
+        from_other(yy)
+        features(yy * 2 + zh)
 
     def from_other_far(yy):
         piece = w_rows(yy, lo, 1 - c)
@@ -402,19 +417,21 @@
         before = yy
     from_other_far(before)
 
+    rinv = rinv_ref[:, :1]
+    factor = jnp.sum(dot_ref[...], axis=1, keepdims=True) * (1.0 / width) * rinv * rinv
+    dot_ref[...] = jnp.broadcast_to(factor, dot_ref.shape)
+
     def finish(i, carry):
         at = pl.ds(pl.multiple_of(i * 16, 16), 16)
-        rinv = rinv_ref[at][:, :1]
-        factor = jnp.sum(dot_ref[at], axis=1, keepdims=True) * (1.0 / width) * rinv * rinv
-        out[at] = ((scaled[at] - res[at].astype(F32) * factor) * rinv).astype(BF16)
+        rinv, factor = rinv_ref[at], dot_ref[at]
+        for k in range(width // BLOCK):
+            lanes = slice(k * BLOCK, (k + 1) * BLOCK)
+            out[at, lanes] = (
+                (scaled[at, lanes] - res[at, lanes].astype(F32) * factor) * rinv
+            ).astype(BF16)
         return carry
 
-    stores = []
-    for k in range(4):
-        part = pl.ds(k * (tokens // 4), tokens // 4)
-        lax.fori_loop(k * (tokens // 64), (k + 1) * (tokens // 64), finish, 0)
-        stores.append(pltpu.make_async_copy(out.at[part], out_hbm.at[part], out_sem.at[k]))
-        stores[-1].start()
+    lax.fori_loop(0, tokens // 16, finish, 0)
 
     place_of_rows = (lax.axis_index("node") * (RING * Z_LO) + lax.axis_index("group")) * rows
     lane = lax.broadcasted_iota(jnp.int32, (16, width), 1)
@@ -429,11 +446,15 @@
     total = send3[z].astype(F32)
     for k in range(DEPTH - 1):
         total = total + recv3[k].astype(F32)
-    wg_ref[...] = (total * (own_gain * scale))[:rows]
+    packed[0] = total
+    factor = (own_gain * scale)[:rows]
+    wg_ref[:, :wide] = packed[0, :rows] * factor
+    wg_ref[:high, wide:] = packed[0, rows:, :BLOCK] * factor[:high]
+    wg_ref[high:, wide:] = packed[0, rows : 2 * rows - high, BLOCK : 2 * BLOCK] * factor[high:]
 
     swap_grad.wait_send()
     for b in range(8):
-        swap_res[b].wait_send()
+        swap_res(b).wait_send()
     @pl.when(sends_far)
     def _():
         for j in range(REACH):
@@ -463,8 +484,6 @@
         to_other_far(yy).wait_send()
     for d in distances:
         copy_three(d).wait_send()
-    for store in stores:
-        store.wait()
 
 
 def on_device(residual, norm_gain_vector, key_projection_matrix, key_output_gradient):
@@ -481,25 +500,25 @@
             pltpu.VMEM((shard // (RING * Z_LO), features), F32),
         ),
         in_specs=[hbm, hbm, hbm, vmem],
-        out_specs=(pl.BlockSpec(memory_space=pl.ANY), vmem),
+        out_specs=(vmem, vmem),
         scratch_shapes=[
             pltpu.VMEM((tokens, width), BF16),
             pltpu.VMEM((tokens, features), BF16),
             pltpu.VMEM((8, 2 * tokens, 384), BF16),
             pltpu.VMEM((2 * tokens, features), BF16),
-            pltpu.VMEM((384, features), F32),
+            pltpu.VMEM((8, 384, 2 * tokens), BF16),
             pltpu.VMEM((RING, RING, 2 * quarter, features), BF16),
             pltpu.VMEM((3, RING, 2 * quarter, features), BF16),
             pltpu.VMEM((RING, 2 * quarter, features), BF16),
             pltpu.VMEM((3, 2 * quarter, features), BF16),
-            pltpu.VMEM((2 * quarter + 16, features), F32),
-            pltpu.VMEM((DEPTH, 16, features), BF16),
-            pltpu.VMEM((DEPTH - 1, 16, features), BF16),
+            pltpu.VMEM((2 * quarter, features), F32),
+            pltpu.VMEM((DEPTH, 16, features - BLOCK), F32),
+            pltpu.VMEM((DEPTH, 16, features - BLOCK), BF16),
+            pltpu.VMEM((DEPTH - 1, 16, features - BLOCK), BF16),
             pltpu.VMEM((width, features), BF16),
             pltpu.VMEM((tokens, width), F32),
             pltpu.VMEM((tokens, 128), F32),
             pltpu.VMEM((tokens, 128), F32),
-            pltpu.VMEM((tokens, width), BF16),
             pltpu.SemaphoreType.DMA((11,)),
             pltpu.SemaphoreType.DMA((2, 9)),
             pltpu.SemaphoreType.DMA((2, 3, RING)),
@@ -513,7 +532,6 @@
             pltpu.SemaphoreType.DMA((2, 3, RING)),
             pltpu.SemaphoreType.DMA((2, RING)),
             pltpu.SemaphoreType.DMA((2, RING)),
-            pltpu.SemaphoreType.DMA((4,)),
         ],
         compiler_params=pltpu.CompilerParams(
             collective_id=0, has_side_effects=True, vmem_limit_bytes=54 * 2**20

time: 63.6 us -> 60.2 us (0.947); the launches traced: 62.8 us -> 60.1 us
  Pallas kernels: 60.3 us -> 57.5 us
    pallas_call x1, Pallas kernels: 60.3 us -> 57.5 us  [on_device(): pl.pallas_call(kernel, out_shape=(pltpu.VMEM((tokens, width), BF16), pltp...]
where the time goes in v4:
time: 60.2 us; the launch traced here: 60.1 us
  Pallas kernels  57.5 us (96%)
  local copies, waits for them, and re-layouts  1.89 us (3%)
  between operations  0.64 us (1%)
    pallas_call x1, Pallas kernels, on_device(): pl.pallas_call(kernel, out_shape=(pltpu.VMEM((tokens, width), BF16), pltp...  57.5 us
    unnamed x2, local copies, waits for them, and re-layouts  1.89 us

profile of v4, /device:TPU:1, one launch (start us, length us, event | category | flops | bytes accessed | tf_op | source)
XLA Modules:
  0.0 60.1 jit_solution(15519585016485221057)
XLA Ops:
  0.6 57.5 %key_backward.1 = (bf16[192,5120]{1,0:T(8,128)(2,1)S(1)}, f32[10,512]{1,0:T(8,128)S(1)}) custom-call(bf16[192,5120]{1,0:T(8,128)(2,1)} %res_hbm.1, bf16[192,512]{1,0:T(8,128)(2,1)} %grad_hbm.1, bf16[320,512]{1,0:T(8,128)(2,1)} %w_hbm.1, f32[1,5120]{1,0:T(1,128)} %bitcast.1), custom_call_target="tpu_custom_call" | custom-call | tf_op jit(solution)/shard_map/key_backward/pallas_call | solution.py:496
  58.2 1.3 %copy.8 = bf16[192,5120]{1,0:T(8,128)(2,1)} copy(bf16[192,5120]{1,0:T(8,128)(2,1)S(1)} %get-tuple-element.2) | data formatting | bytes 3932160
  59.4 0.6 %copy.9 = f32[10,512]{1,0:T(8,128)} copy(f32[10,512]{1,0:T(8,128)S(1)} %get-tuple-element.3) | data formatting | bytes 40960

commit v5 on v4

--- a/solution.py
+++ b/solution.py
@@ -224,10 +224,42 @@
     lax.fori_loop(0, 8, turn, 0)
     swap_grad.wait_recv()
 
-    def copy_one(d, s):
+    halves = (pl.ds(0, quarter), pl.ds(quarter, quarter))
+    up, down, opposite = (first + 1) % RING, (first + 3) % RING, (first + 2) % RING
+
+    def hop(k, s):
+        block, slot, half, target = (
+            (opposite, 2, 0, 1),
+            (opposite, 2, 1, 3),
+            (up, 0, 1, 1),
+            (down, 1, 0, 3),
+            (up, 0, 0, 1),
+            (down, 1, 1, 3),
+        )[k]
         return remote(
-            send1.at[(first + d) % RING, s], recv1.at[d - 1, s], one_sem, (d - 1, s), along_first(d)
+            send1.at[block, s, halves[half]],
+            recv1.at[slot, s, halves[half]],
+            one_sem,
+            (k, s),
+            along_first(target),
         )
+
+    def relay(s):
+        hop(0, s).wait_recv()
+        hop(1, s).wait_recv()
+
+        def join(i, carry):
+            low = pl.ds(pl.multiple_of(i * 16, 16), 16)
+            high = pl.ds(pl.multiple_of(quarter + i * 16, 16), 16)
+            send1[up, s, low] = (send1[up, s, low].astype(F32) + recv1[2, s, low].astype(F32)).astype(BF16)
+            send1[down, s, high] = (
+                send1[down, s, high].astype(F32) + recv1[2, s, high].astype(F32)
+            ).astype(BF16)
+            return carry
+
+        lax.fori_loop(0, quarter // 16, join, 0)
+        hop(4, s).start()
+        hop(5, s).start()
 
     def partial_block(yy):
         def half(hi, carry):
@@ -250,14 +282,14 @@
 
         @pl.when(c == 0)
         def _(yy=yy):
-            for d in (2, 1, 3):
-                copy_one(d, yy).start()
-
-    @pl.when(c == 1)
-    def _():
-        for step in ORDER:
-            for d in (2, 1, 3):
-                copy_one(d, (x + step) % RING).start()
+            for k in range(4):
+                hop(k, yy).start()
+
+        @pl.when(c == 1)
+        def _(step=step):
+            for other_step in ORDER:
+                for k in {2: (0, 1), 1: (2,), 3: (3,), 0: ()}[step]:
+                    hop(k, (x + other_step) % RING).start()
 
     for d in (1, 3, 2):
         w_near(d).wait_recv()
@@ -305,15 +337,18 @@
             for d in (1, 3, 2):
                 w_whole(d).start()
 
-    for step in ORDER:
+    relay((second + ORDER[0]) % RING)
+    for place_in_order, step in enumerate(ORDER):
         s = (second + step) % RING
-        for d in (1, 2, 3):
-            copy_one(d, s).wait_recv()
+        if place_in_order < RING - 1:
+            relay((second + ORDER[place_in_order + 1]) % RING)
+        for k in range(2, 6):
+            hop(k, s).wait_recv()
 
         def add(i, carry, s=s, step=step):
             at = pl.ds(pl.multiple_of(i * 16, 16), 16)
             total = send1[first, s, at].astype(F32)
-            for k in range(3):
+            for k in range(2):
                 total = total + recv1[k, s, at].astype(F32)
             if step:
                 red[s, at] = total.astype(BF16)
@@ -466,7 +501,8 @@
         w_side(d).wait_send()
         copy_two(d).wait_send()
         for s in range(RING):
-            copy_one(d, s).wait_send()
+            hop(d - 1, s).wait_send()
+            hop(d + 2, s).wait_send()
 
     @pl.when(c == 0)
     def _():
@@ -521,7 +557,7 @@
             pltpu.VMEM((tokens, 128), F32),
             pltpu.SemaphoreType.DMA((11,)),
             pltpu.SemaphoreType.DMA((2, 9)),
-            pltpu.SemaphoreType.DMA((2, 3, RING)),
+            pltpu.SemaphoreType.DMA((2, 6, RING)),
             pltpu.SemaphoreType.DMA((2, 3)),
             pltpu.SemaphoreType.DMA((2, DEPTH - 1)),
             pltpu.SemaphoreType.REGULAR((3,)),

time: 60.2 us -> 58.4 us (0.970)
  Pallas kernels: 57.5 us -> 55.7 us
    pallas_call x1, Pallas kernels: 57.5 us -> 55.7 us  [on_device(): pl.pallas_call(kernel, out_shape=(pltpu.VMEM((tokens, width), BF16), pltp...]
where the time goes in v5:
time: 58.4 us; the launch traced here: 58.2 us
  Pallas kernels  55.7 us (95%)
  local copies, waits for them, and re-layouts  1.89 us (3%)
  between operations  0.64 us (1%)
    pallas_call x1, Pallas kernels, on_device(): pl.pallas_call(kernel, out_shape=(pltpu.VMEM((tokens, width), BF16), pltp...  55.7 us
    unnamed x2, local copies, waits for them, and re-layouts  1.89 us

profile of v5, /device:TPU:1, one launch (start us, length us, event | category | flops | bytes accessed | tf_op | source)
XLA Modules:
  0.0 58.2 jit_solution(1604011940120513346)
XLA Ops:
  0.6 55.7 %key_backward.1 = (bf16[192,5120]{1,0:T(8,128)(2,1)S(1)}, f32[10,512]{1,0:T(8,128)S(1)}) custom-call(bf16[192,5120]{1,0:T(8,128)(2,1)} %res_hbm.1, bf16[192,512]{1,0:T(8,128)(2,1)} %grad_hbm.1, bf16[320,512]{1,0:T(8,128)(2,1)} %w_hbm.1, f32[1,5120]{1,0:T(1,128)} %bitcast.1), custom_call_target="tpu_custom_call" | custom-call | tf_op jit(solution)/shard_map/key_backward/pallas_call | solution.py:532
  56.3 1.3 %copy.8 = bf16[192,5120]{1,0:T(8,128)(2,1)} copy(bf16[192,5120]{1,0:T(8,128)(2,1)S(1)} %get-tuple-element.2) | data formatting | bytes 3932160
  57.6 0.6 %copy.9 = f32[10,512]{1,0:T(8,128)} copy(f32[10,512]{1,0:T(8,128)S(1)} %get-tuple-element.3) | data formatting | bytes 40960

commit v6 on v5

--- a/solution.py
+++ b/solution.py
@@ -104,9 +104,6 @@
         + [along_y(d) for d in (1, 2, 3)]
         + [other]
     )
-    for partner in partners:
-        pl.semaphore_signal(barrier, inc=1, device_id=partner, device_id_type=MESH)
-
     def w_rows(yy, hi, core, count=shard, at=0):
         start = ((yy * 2 + hi) * 2 + core) * shard + at
         return w.at[pl.ds(pl.multiple_of(start, 16), count)]
@@ -123,8 +120,10 @@
     def load_pair(b):
         return pltpu.make_async_copy(columns(b, c), both_res.at[b, mine], local_sem.at[3 + b])
 
+    load_grad.start()
     load_res.start()
-    load_grad.start()
+    for partner in partners:
+        pl.semaphore_signal(barrier, inc=1, device_id=partner, device_id_type=MESH)
     for b in range(8):
         load_pair(b).start()
     load_w.start()
@@ -206,14 +205,16 @@
             device_id_type=MESH,
         )
 
-    hear(1)
-
-    @pl.when(sends_far)
-    def _():
-        for j in range(REACH - 1, -1, -1):
-            w_far(j).start()
-
-    tell(2)
+    def far_out():
+        hear(1)
+
+        @pl.when(sends_far)
+        def _():
+            for j in range(REACH - 1, -1, -1):
+                w_far(j).start()
+
+        tell(2)
+
 
     def turn(b, carry):
         load_pair(b).wait()
@@ -291,6 +292,9 @@
                 for k in {2: (0, 1), 1: (2,), 3: (3,), 0: ()}[step]:
                     hop(k, (x + other_step) % RING).start()
 
+        if step == 2:
+            far_out()
+
     for d in (1, 3, 2):
         w_near(d).wait_recv()
         w_swap(d).start()
@@ -359,7 +363,7 @@
         lax.fori_loop(0, 2 * quarter // 16, add, 0)
         if step:
             copy_two(step).start()
-        if step == 1:
+        if step == 2:
             first_part()
         if step == 3:
             second_part()

time: 58.4 us -> 57 us (0.976)
  Pallas kernels: 55.7 us -> 54.2 us
    pallas_call x1, Pallas kernels: 55.7 us -> 54.2 us  [on_device(): pl.pallas_call(kernel, out_shape=(pltpu.VMEM((tokens, width), BF16), pltp...]
where the time goes in v6:
time: 57 us; the launch traced here: 56.8 us
  Pallas kernels  54.2 us (95%)
  local copies, waits for them, and re-layouts  1.89 us (3%)
  between operations  0.64 us (1%)
    pallas_call x1, Pallas kernels, on_device(): pl.pallas_call(kernel, out_shape=(pltpu.VMEM((tokens, width), BF16), pltp...  54.2 us
    unnamed x2, local copies, waits for them, and re-layouts  1.89 us

profile of v6, /device:TPU:1, one launch (start us, length us, event | category | flops | bytes accessed | tf_op | source)
XLA Modules:
  0.0 56.8 jit_solution(2553181755403205924)
XLA Ops:
  0.6 54.2 %key_backward.1 = (bf16[192,5120]{1,0:T(8,128)(2,1)S(1)}, f32[10,512]{1,0:T(8,128)S(1)}) custom-call(bf16[192,5120]{1,0:T(8,128)(2,1)} %res_hbm.1, bf16[192,512]{1,0:T(8,128)(2,1)} %grad_hbm.1, bf16[320,512]{1,0:T(8,128)(2,1)} %w_hbm.1, f32[1,5120]{1,0:T(1,128)} %bitcast.1), custom_call_target="tpu_custom_call" | custom-call | tf_op jit(solution)/shard_map/key_backward/pallas_call | solution.py:536
  54.9 1.3 %copy.8 = bf16[192,5120]{1,0:T(8,128)(2,1)} copy(bf16[192,5120]{1,0:T(8,128)(2,1)S(1)} %get-tuple-element.2) | data formatting | bytes 3932160
  56.2 0.6 %copy.9 = f32[10,512]{1,0:T(8,128)} copy(f32[10,512]{1,0:T(8,128)S(1)} %get-tuple-element.3) | data formatting | bytes 40960

commit v7 on v6

--- a/solution.py
+++ b/solution.py
@@ -295,9 +295,6 @@
         if step == 2:
             far_out()
 
-    for d in (1, 3, 2):
-        w_near(d).wait_recv()
-        w_swap(d).start()
 
     lo = 1 - zh
 
@@ -342,6 +339,9 @@
                 w_whole(d).start()
 
     relay((second + ORDER[0]) % RING)
+    for d in (1, 3, 2):
+        w_near(d).wait_recv()
+        w_swap(d).start()
     for place_in_order, step in enumerate(ORDER):
         s = (second + step) % RING
         if place_in_order < RING - 1:
@@ -350,7 +350,7 @@
             hop(k, s).wait_recv()
 
         def add(i, carry, s=s, step=step):
-            at = pl.ds(pl.multiple_of(i * 16, 16), 16)
+            at = pl.ds(pl.multiple_of(i * quarter, 16), quarter)
             total = send1[first, s, at].astype(F32)
             for k in range(2):
                 total = total + recv1[k, s, at].astype(F32)
@@ -360,7 +360,7 @@
                 acc[at] = total
             return carry
 
-        lax.fori_loop(0, 2 * quarter // 16, add, 0)
+        lax.fori_loop(0, 2, add, 0)
         if step:
             copy_two(step).start()
         if step == 2:
@@ -398,14 +398,14 @@
         copy_two(e).wait_recv()
 
     def add_two(i, carry):
-        at = pl.ds(pl.multiple_of(i * 16, 16), 16)
+        at = pl.ds(pl.multiple_of(i * quarter, 16), quarter)
         total = acc[at]
         for k in range(3):
             total = total + recv2[k, at].astype(F32)
         acc[at] = total
         return carry
 
-    lax.fori_loop(0, 2 * quarter // 16, add_two, 0)
+    lax.fori_loop(0, 2, add_two, 0)
     high, wide = 16 - rows, acc.shape[1] - BLOCK
     for k in range(DEPTH):
         at = k * rows

time: 57 us -> 56.7 us (level)
  no operation moved by 1% of the time
where the time goes in v7:
time: 56.7 us; the launch traced here: 56.5 us
  Pallas kernels  54 us (95%)
  local copies, waits for them, and re-layouts  1.89 us (3%)
  between operations  0.64 us (1%)
    pallas_call x1, Pallas kernels, on_device(): pl.pallas_call(kernel, out_shape=(pltpu.VMEM((tokens, width), BF16), pltp...  54 us
    unnamed x2, local copies, waits for them, and re-layouts  1.89 us

profile of v7, /device:TPU:1, one launch (start us, length us, event | category | flops | bytes accessed | tf_op | source)
XLA Modules:
  0.0 56.5 jit_solution(1021036590819322579)
XLA Ops:
  0.6 54.0 %key_backward.1 = (bf16[192,5120]{1,0:T(8,128)(2,1)S(1)}, f32[10,512]{1,0:T(8,128)S(1)}) custom-call(bf16[192,5120]{1,0:T(8,128)(2,1)} %res_hbm.1, bf16[192,512]{1,0:T(8,128)(2,1)} %grad_hbm.1, bf16[320,512]{1,0:T(8,128)(2,1)} %w_hbm.1, f32[1,5120]{1,0:T(1,128)} %bitcast.1), custom_call_target="tpu_custom_call" | custom-call | tf_op jit(solution)/shard_map/key_backward/pallas_call | solution.py:536
  54.7 1.3 %copy.8 = bf16[192,5120]{1,0:T(8,128)(2,1)} copy(bf16[192,5120]{1,0:T(8,128)(2,1)S(1)} %get-tuple-element.2) | data formatting | bytes 3932160
  55.9 0.6 %copy.9 = f32[10,512]{1,0:T(8,128)} copy(f32[10,512]{1,0:T(8,128)S(1)} %get-tuple-element.3) | data formatting | bytes 40960
